TPU v7x, 1024 devices: a whole 4x8x16 slice. The times are simulated.
1024 devices in a mesh: expert: 16 (over y, core), replica: 64 (over x, z).
Axes of the slice: x: 4, y: 8, z: 16, core: 2. Of those that a mesh axis runs over, the one named last changes fastest.
Arguments:
- hidden_in: bfloat16 [1024, 3584], P('replica'), may hold values from -6 to 6
- norm_gain: float32 [3584], replicated, may hold values from 0.5 to 1.5
- expert_ids: int32 [1024, 8], P('replica'), may hold values from 0 to 63, all different within a row; in each aligned block of 16 rows (0 to 15, 16 to 31, ...) at most 4 rows name the same one
- gate_scores: int32 [1024, 8], P('replica'), may hold values from 1 to 64
- w_gate: bfloat16 [64, 1024, 3584], P('replica', 'expert'), may hold values from -0.09375 to 0.09375
- w_up: bfloat16 [64, 1024, 3584], P('replica', 'expert'), may hold values from -0.09375 to 0.09375
- w_down: bfloat16 [64, 1024, 3584], P('replica', 'expert'), may hold values from -0.1875 to 0.1875
- shared_gate: bfloat16 [1024, 3584], P('expert'), may hold values from -0.09375 to 0.09375
- shared_up: bfloat16 [1024, 3584], P('expert'), may hold values from -0.09375 to 0.09375
- shared_down: bfloat16 [1024, 3584], P('expert'), may hold values from -0.1875 to 0.1875
- out_grad: bfloat16 [1024, 3584], P('replica'), may hold values from -6 to 6
Outputs:
- moe_out: bfloat16 [1024, 3584], P('replica')
- hidden_grad: bfloat16 [1024, 3584], P('replica')
- gain_grad: float32 [3584], P('replica')
- gate_grad: bfloat16 [64, 1024, 3584], P('replica', 'expert')
- up_grad: bfloat16 [64, 1024, 3584], P('replica', 'expert')
- down_grad: bfloat16 [64, 1024, 3584], P('replica', 'expert')
- shared_gate_grad: bfloat16 [1024, 3584], P('expert', 'replica')
- shared_up_grad: bfloat16 [1024, 3584], P('expert', 'replica')
- shared_down_grad: bfloat16 [1024, 3584], P('expert', 'replica')
Inputs may be any that keep to these rules, and one draw needn't show every extreme that they name: `expert_ids`: each row names 8 different experts; within the rows of one replica index (aligned blocks of 16 rows) no expert is named more than 4 times, a bound that some block reaches.
All inputs are finite; a program needn't handle non-finite values.
Results may differ from a plain program's by a relative error of at most 0.024.
Values may be sent and summed in bfloat16 or wider, within the bound.
A program may use at most 64 MiB of HBM per device.

v0:
```python
import jax
import jax.numpy as jnp
from jax import lax
from jax.sharding import PartitionSpec as P


def silu_slope(values):
    sigmoid_v = jax.nn.sigmoid(values)
    return sigmoid_v * (1.0 + values * (1.0 - sigmoid_v))


def inner_rows(left, right):
    return lax.dot_general(
        left, right, (((0,), (0,)), ((), ())), preferred_element_type=jnp.float32
    )


def times_transposed(left, right):
    return lax.dot_general(
        left, right, (((1,), (1,)), ((), ())), preferred_element_type=jnp.float32
    )


def per_device(
    hidden_in,
    norm_gain,
    expert_ids,
    gate_scores,
    w_gate,
    w_up,
    w_down,
    shared_gate,
    shared_up,
    shared_down,
    out_grad,
):
    tok_rows, model_width = hidden_in.shape
    fanout = expert_ids.shape[1]
    groups = lax.axis_size("replica")
    capacity = min(tok_rows, max(2, tok_rows * fanout * 2 // groups))
    widened = hidden_in.astype(jnp.float32)
    inv_rms = lax.rsqrt(jnp.mean(widened * widened, axis=-1, keepdims=True) + 1e-06)
    normalized = widened * inv_rms
    normed = (normalized * norm_gain).astype(jnp.bfloat16)
    scores = gate_scores.astype(jnp.float32)
    gate_weights = 2.5 * scores / jnp.sum(scores, axis=-1, keepdims=True)
    pair_ids = expert_ids.reshape(-1)
    onehot = (pair_ids[:, None] == jnp.arange(groups, dtype=jnp.int32)[None, :]).astype(jnp.int32)
    earlier = jnp.cumsum(onehot, axis=0) - onehot
    ranking = jnp.sum(earlier * onehot, axis=1)
    slot_index = pair_ids * capacity + ranking
    placing = (
        slot_index[:, None] == jnp.arange(groups * capacity, dtype=jnp.int32)[None, :]
    ).astype(jnp.bfloat16)
    repeated = jnp.repeat(normed, fanout, axis=0)
    scaled_grad = (
        (gate_weights[:, :, None] * out_grad.astype(jnp.float32)[:, None, :])
        .astype(jnp.bfloat16)
        .reshape(-1, model_width)
    )
    send_rows = (
        inner_rows(placing, repeated).astype(jnp.bfloat16).reshape(groups, capacity, model_width)
    )
    send_cots = (
        inner_rows(placing, scaled_grad).astype(jnp.bfloat16).reshape(groups, capacity, model_width)
    )
    recv_rows, recv_cots = (
        lax.all_to_all(send_rows, "replica", split_axis=0, concat_axis=0, tiled=True),
        lax.all_to_all(send_cots, "replica", split_axis=0, concat_axis=0, tiled=True),
    )
    rows_in = recv_rows.reshape(groups * capacity, model_width)
    cot_rows = recv_cots.reshape(groups * capacity, model_width)
    gate_mat = w_gate[0]
    up_mat = w_up[0]
    down_mat = w_down[0]
    pre_gate = times_transposed(rows_in, gate_mat)
    pre_up = times_transposed(rows_in, up_mat)
    activation = (jax.nn.silu(pre_gate) * pre_up).astype(jnp.bfloat16)
    part_out = jnp.dot(activation, down_mat, preferred_element_type=jnp.float32).astype(
        jnp.bfloat16
    )
    act_grad = times_transposed(cot_rows, down_mat)
    gate_delta = (act_grad * pre_up * silu_slope(pre_gate)).astype(jnp.bfloat16)
    up_delta = (act_grad * jax.nn.silu(pre_gate)).astype(jnp.bfloat16)
    part_in = (
        jnp.dot(gate_delta, gate_mat, preferred_element_type=jnp.float32)
        + jnp.dot(up_delta, up_mat, preferred_element_type=jnp.float32)
    ).astype(jnp.bfloat16)
    gate_grad = inner_rows(gate_delta, rows_in).astype(jnp.bfloat16)[None]
    up_grad = inner_rows(up_delta, rows_in).astype(jnp.bfloat16)[None]
    down_grad = inner_rows(activation, cot_rows).astype(jnp.bfloat16)[None]
    back_out, back_in = (
        lax.all_to_all(
            part_out.reshape(groups, capacity, model_width),
            "replica",
            split_axis=0,
            concat_axis=0,
            tiled=True,
        ),
        lax.all_to_all(
            part_in.reshape(groups, capacity, model_width),
            "replica",
            split_axis=0,
            concat_axis=0,
            tiled=True,
        ),
    )
    pair_out = jnp.dot(
        placing,
        back_out.reshape(groups * capacity, model_width),
        preferred_element_type=jnp.float32,
    ).reshape(tok_rows, fanout, model_width)
    pair_in = jnp.dot(
        placing, back_in.reshape(groups * capacity, model_width), preferred_element_type=jnp.float32
    ).reshape(tok_rows, fanout, model_width)
    routed_out = jnp.sum(gate_weights[:, :, None] * pair_out, axis=1)
    routed_in = jnp.sum(pair_in, axis=1)
    shared_pre_gate = times_transposed(normed, shared_gate)
    shared_pre_up = times_transposed(normed, shared_up)
    shared_act = (jax.nn.silu(shared_pre_gate) * shared_pre_up).astype(jnp.bfloat16)
    shared_out = jnp.dot(shared_act, shared_down, preferred_element_type=jnp.float32)
    shared_act_grad = times_transposed(out_grad, shared_down)
    shared_gate_delta = (shared_act_grad * shared_pre_up * silu_slope(shared_pre_gate)).astype(
        jnp.bfloat16
    )
    shared_up_delta = (shared_act_grad * jax.nn.silu(shared_pre_gate)).astype(jnp.bfloat16)
    shared_in = jnp.dot(
        shared_gate_delta, shared_gate, preferred_element_type=jnp.float32
    ) + jnp.dot(shared_up_delta, shared_up, preferred_element_type=jnp.float32)
    token_total, normed_grad = (
        lax.psum((routed_out + shared_out).astype(jnp.bfloat16), "expert").astype(jnp.float32),
        lax.psum((routed_in + shared_in).astype(jnp.bfloat16), "expert").astype(jnp.float32),
    )
    moe_out = token_total.astype(jnp.bfloat16)
    scaled = normed_grad * norm_gain
    hidden_grad = (
        inv_rms * (scaled - normalized * jnp.mean(scaled * normalized, axis=-1, keepdims=True))
    ).astype(jnp.bfloat16)
    gain_terms = normed_grad * normalized
    token_cols, grad_cols = (
        lax.all_to_all(normed, "replica", split_axis=1, concat_axis=0, tiled=True),
        lax.all_to_all(out_grad, "replica", split_axis=1, concat_axis=0, tiled=True),
    )
    every_gate, every_up, every_act = (
        lax.all_gather(shared_gate_delta, "replica", axis=0, tiled=True),
        lax.all_gather(shared_up_delta, "replica", axis=0, tiled=True),
        lax.all_gather(shared_act, "replica", axis=0, tiled=True),
    )
    gain_cols = lax.all_to_all(
        gain_terms.astype(jnp.bfloat16), "replica", split_axis=1, concat_axis=0, tiled=True
    ).astype(gain_terms.dtype)
    summed_gate = inner_rows(every_gate, token_cols)
    summed_up = inner_rows(every_up, token_cols)
    summed_down = inner_rows(every_act, grad_cols)
    gain_grad = jnp.sum(gain_cols, axis=0)
    return (
        moe_out,
        hidden_grad,
        gain_grad,
        gate_grad,
        up_grad,
        down_grad,
        summed_gate.astype(jnp.bfloat16),
        summed_up.astype(jnp.bfloat16),
        summed_down.astype(jnp.bfloat16),
    )


def solution(mesh):
    in_specs = (
        P("replica", None),
        P(),
        P("replica", None),
        P("replica", None),
        P("replica", "expert", None),
        P("replica", "expert", None),
        P("replica", "expert", None),
        P("expert", None),
        P("expert", None),
        P("expert", None),
        P("replica", None),
    )
    out_specs = (
        P("replica", None),
        P("replica", None),
        P("replica"),
        P("replica", "expert", None),
        P("replica", "expert", None),
        P("replica", "expert", None),
        P("expert", "replica"),
        P("expert", "replica"),
        P("expert", "replica"),
    )
    return jax.shard_map(
        per_device, mesh=mesh, in_specs=in_specs, out_specs=out_specs, check_vma=False
    )
```

profile of v0, /device:TPU:1, one launch (start us, length us, event | category | flops | bytes accessed | tf_op | source)
XLA Modules:
  0.0 883.1 jit_solution(17140472797649877866)
XLA Ops:
  11.7 0.9 convert_element_type.99
  13.4 1.5 reshape.128
  14.9 22.9 %all-to-all-start.2 = ((bf16[64,4,3584]{2,1,0:T(4,128)(2,1)}), bf16[64,4,3584]{2,1,0:T(4,128)(2,1)S(1)}, u32[]{:S(2)}, u32[]{:S(2)}) async-start(bf16[64,4,3584]{2,1,0:T(4,128)(2,1)} %reshape.128), calls=%async_computation.2 | async-start | bytes 3670016 | tf_op jit(solution)/shard_map/all_to_all | solution.py:69
  38.1 2.0 convolution_convert_fusion.1
  40.1 4.1 reshape.124
  44.2 74.8 %all-to-all-done.2 = bf16[64,4,3584]{2,1,0:T(4,128)(2,1)S(1)} async-done(((bf16[64,4,3584]{2,1,0:T(4,128)(2,1)}), bf16[64,4,3584]{2,1,0:T(4,128)(2,1)S(1)}, u32[]{:S(2)}, u32[]{:S(2)}) %all-to-all-start.2) | async-done | bytes 1835040 | tf_op jit(solution)/shard_map/all_to_all | solution.py:69
  118.9 13.5 %all-to-all-start = ((bf16[64,4,3584]{2,1,0:T(4,128)(2,1)}), bf16[64,4,3584]{2,1,0:T(4,128)(2,1)}, u32[]{:S(2)}, u32[]{:S(2)}) async-start(bf16[64,4,3584]{2,1,0:T(4,128)(2,1)} %reshape.124), calls=%async_computation | async-start | bytes 3670016 | tf_op jit(solution)/shard_map/all_to_all | solution.py:68
  133.7 1.0 reshape.138
  134.8 1.0 reshape.140
  135.8 1.5 reshape.129
  137.3 76.7 %all-to-all-done = bf16[64,4,3584]{2,1,0:T(4,128)(2,1)} async-done(((bf16[64,4,3584]{2,1,0:T(4,128)(2,1)}), bf16[64,4,3584]{2,1,0:T(4,128)(2,1)}, u32[]{:S(2)}, u32[]{:S(2)}) %all-to-all-start) | async-done | bytes 1835040 | tf_op jit(solution)/shard_map/all_to_all | solution.py:68
  214.0 12.8 %all-to-all-start.5 = ((bf16[64,2,448]{2,1,0:T(2,128)(2,1)}), bf16[64,2,448]{2,1,0:T(2,128)(2,1)S(1)}, u32[]{:S(2)}, u32[]{:S(2)}) async-start(bf16[64,2,448]{2,1,0:T(2,128)(2,1)} %reshape.138), calls=%async_computation.5 | async-start | bytes 262144 | tf_op jit(solution)/shard_map/all_to_all | solution.py:141
  226.8 3.0 reshape.125
  230.9 1.3 fusion.21
  232.2 8.8 all-to-all-done.5
  241.0 7.4 all-to-all-start.6
  248.4 2.2 multiply_convert_fusion
  250.6 1.9 convolution_convert_fusion.2
  252.5 4.1 reshape.126
  256.6 5.8 all-to-all-done.6
  263.0 9.2 %all-to-all-start.1 = ((bf16[64,4,3584]{2,1,0:T(4,128)(2,1)}), bf16[64,4,3584]{2,1,0:T(4,128)(2,1)}, u32[]{:S(2)}, u32[]{:S(2)}) async-start(bf16[64,4,3584]{2,1,0:T(4,128)(2,1)} %reshape.126), calls=%async_computation.1 | async-start | bytes 3670016 | tf_op jit(solution)/shard_map/all_to_all | solution.py:93
  272.2 1.7 fusion.19
  273.9 2.0 fusion
  275.9 4.1 reshape.130
  280.0 72.5 %all-to-all-done.1 = bf16[64,4,3584]{2,1,0:T(4,128)(2,1)} async-done(((bf16[64,4,3584]{2,1,0:T(4,128)(2,1)}), bf16[64,4,3584]{2,1,0:T(4,128)(2,1)}, u32[]{:S(2)}, u32[]{:S(2)}) %all-to-all-start.1) | async-done | bytes 1835040 | tf_op jit(solution)/shard_map/all_to_all | solution.py:93
  352.4 13.8 %all-to-all-start.3 = ((bf16[64,4,3584]{2,1,0:T(4,128)(2,1)}), bf16[64,4,3584]{2,1,0:T(4,128)(2,1)}, u32[]{:S(2)}, u32[]{:S(2)}) async-start(bf16[64,4,3584]{2,1,0:T(4,128)(2,1)} %reshape.130), calls=%async_computation.3 | async-start | bytes 3670016 | tf_op jit(solution)/shard_map/all_to_all | solution.py:100
  366.4 1.2 fusion.45
  367.7 1.3 fusion.44
  369.2 134.4 %all_gather.9 = bf16[1024,64]{1,0:T(8,128)(2,1)S(1)} all-gather(bf16[16,64]{1,0:T(8,128)(2,1)S(1)} %get-tuple-element.17), channel_id=1, replica_groups=mesh['expert'=16,'replica'=64] {'replica'}, dimensions={0}, use_global_device_ids=true | all-gather | bytes 133120 | tf_op jit(solution)/shard_map/all_gather | solution.py:145
  503.6 68.4 %all_gather.10 = bf16[1024,64]{1,0:T(8,128)(2,1)} all-gather(bf16[16,64]{1,0:T(8,128)(2,1)S(1)} %get-tuple-element.16), channel_id=1, replica_groups=mesh['expert'=16,'replica'=64] {'replica'}, dimensions={0}, use_global_device_ids=true | all-gather | bytes 133120 | tf_op jit(solution)/shard_map/all_gather | solution.py:146
  572.0 69.7 %all_gather.11 = bf16[1024,64]{1,0:T(8,128)(2,1)} all-gather(bf16[16,64]{1,0:T(8,128)(2,1)S(1)} %get-tuple-element.18), channel_id=1, replica_groups=mesh['expert'=16,'replica'=64] {'replica'}, dimensions={0}, use_global_device_ids=true | all-gather | bytes 133120 | tf_op jit(solution)/shard_map/all_gather | solution.py:147
  641.7 1.9 fusion.46
  643.6 1.2 reshape.139
  644.7 1.9 reshape.141
  646.6 1.8 convolution_convert_fusion.7
  649.3 1.9 convolution_convert_fusion.6
  651.1 2.7 fusion.3
  653.8 1.2 fusion.2
  655.1 3.9 reshape.132
  659.0 2.2 fusion.8
  662.1 3.9 reshape.133
  666.0 2.3 convolution_reduce_fusion
  669.2 1.2 fusion.1
  670.4 172.1 %all-reduce.3.cloned.1.call-done = (bf16[16,3584]{1,0:T(8,128)(2,1)}, bf16[16,3584]{1,0:T(8,128)(2,1)}) async-done(((bf16[16,3584]{1,0:T(8,128)(2,1)}, bf16[16,3584]{1,0:T(8,128)(2,1)}), (bf16[16,3584]{1,0:T(8,128)(2,1)}, bf16[16,3584]{1,0:T(8,128)(2,1)})) %all-reduce.3.cloned.1.call-update) | async-done | bytes 229392 | tf_op jit(solution)/shard_map/psum | solution.py:131
  842.5 1.2 fusion.33
  844.4 1.0 reshape.136
  845.3 14.9 %all-to-all-start.4 = ((bf16[64,2,448]{2,1,0:T(2,128)(2,1)}), bf16[64,2,448]{2,1,0:T(2,128)(2,1)S(1)}, u32[]{:S(2)}, u32[]{:S(2)}) async-start(bf16[64,2,448]{2,1,0:T(2,128)(2,1)} %reshape.136), calls=%async_computation.4 | async-start | bytes 262144 | tf_op jit(solution)/shard_map/all_to_all | solution.py:149
  861.0 13.7 %all-to-all-done.4 = bf16[64,2,448]{2,1,0:T(2,128)(2,1)S(1)} async-done(((bf16[64,2,448]{2,1,0:T(2,128)(2,1)}), bf16[64,2,448]{2,1,0:T(2,128)(2,1)S(1)}, u32[]{:S(2)}, u32[]{:S(2)}) %all-to-all-start.4) | async-done | bytes 114720 | tf_op jit(solution)/shard_map/all_to_all | solution.py:149
  (93 shorter events, 14.5 us)
Async XLA Ops:
  7.2 241.2 %copy-start = (bf16[1,64,3584]{2,1,0:T(8,128)(2,1)S(1)}, bf16[1,64,3584]{2,1,0:T(8,128)(2,1)}, u32[]{:S(2)}) copy-start(bf16[1,64,3584]{2,1,0:T(8,128)(2,1)} %param.17) | copy-start | bytes 1376260
  8.7 0.6 copy-start.23
  10.2 0.6 copy-start.17
  11.2 0.5 copy-start.27
  14.9 22.9 %copy-start.3 = (bf16[16,3584]{1,0:T(8,128)(2,1)S(1)}, bf16[16,3584]{1,0:T(8,128)(2,1)}, u32[]{:S(2)}) copy-start(bf16[16,3584]{1,0:T(8,128)(2,1)} %param.11) | copy-start | bytes 344068
  14.9 23.1 %copy-start.15 = (f32[3584]{0:T(1024)S(1)}, f32[3584]{0:T(1024)}, u32[]{:S(2)}) copy-start(f32[3584]{0:T(1024)} %param.12) | copy-start | bytes 43012
  14.9 104.0 %all-to-all-start.2 = ((bf16[64,4,3584]{2,1,0:T(4,128)(2,1)}), bf16[64,4,3584]{2,1,0:T(4,128)(2,1)S(1)}, u32[]{:S(2)}, u32[]{:S(2)}) async-start(bf16[64,4,3584]{2,1,0:T(4,128)(2,1)} %reshape.128), calls=%async_computation.2 | async-start | bytes 3670016 | tf_op jit(solution)/shard_map/all_to_all | solution.py:69
  38.0 6.2 copy-start.25
  44.2 88.8 %copy-start.6 = (bf16[16,3584]{1,0:T(8,128)(2,1)S(1)}, bf16[16,3584]{1,0:T(8,128)(2,1)}, u32[]{:S(2)}) copy-start(bf16[16,3584]{1,0:T(8,128)(2,1)} %param.21) | copy-start | bytes 344068
  118.9 95.0 %all-to-all-start = ((bf16[64,4,3584]{2,1,0:T(4,128)(2,1)}), bf16[64,4,3584]{2,1,0:T(4,128)(2,1)}, u32[]{:S(2)}, u32[]{:S(2)}) async-start(bf16[64,4,3584]{2,1,0:T(4,128)(2,1)} %reshape.124), calls=%async_computation | async-start | bytes 3670016 | tf_op jit(solution)/shard_map/all_to_all | solution.py:68
  214.0 27.0 %all-to-all-start.5 = ((bf16[64,2,448]{2,1,0:T(2,128)(2,1)}), bf16[64,2,448]{2,1,0:T(2,128)(2,1)S(1)}, u32[]{:S(2)}, u32[]{:S(2)}) async-start(bf16[64,2,448]{2,1,0:T(2,128)(2,1)} %reshape.138), calls=%async_computation.5 | async-start | bytes 262144 | tf_op jit(solution)/shard_map/all_to_all | solution.py:141
  226.8 3.0 copy-start.1
  229.8 1.0 copy-start.4
  241.0 11.5 %copy-start.8 = (bf16[64,2,448]{2,1,0:T(2,128)(2,1)}, bf16[64,2,448]{2,1,0:T(2,128)(2,1)S(1)}, u32[]{:S(2)}) copy-start(bf16[64,2,448]{2,1,0:T(2,128)(2,1)S(1)} %all-to-all-done.5) | copy-start | bytes 344068
  241.0 21.3 %all-to-all-start.6 = ((bf16[64,2,448]{2,1,0:T(2,128)(2,1)}), bf16[64,2,448]{2,1,0:T(2,128)(2,1)S(1)}, u32[]{:S(2)}, u32[]{:S(2)}) async-start(bf16[64,2,448]{2,1,0:T(2,128)(2,1)} %reshape.140), calls=%async_computation.6 | async-start | bytes 262144 | tf_op jit(solution)/shard_map/all_to_all | solution.py:142
  250.6 6.0 copy-start.13
  250.6 23.3 %copy-start.11 = (bf16[256,64]{0,1:T(8,128)(2,1)}, bf16[256,64]{0,1:T(8,128)(2,1)S(1)}, u32[]{:S(2)}) copy-start(bf16[256,64]{0,1:T(8,128)(2,1)S(1)} %get-tuple-element.13) | copy-start | bytes 98308
  262.3 0.7 copy-start.9
  263.0 89.5 %all-to-all-start.1 = ((bf16[64,4,3584]{2,1,0:T(4,128)(2,1)}), bf16[64,4,3584]{2,1,0:T(4,128)(2,1)}, u32[]{:S(2)}, u32[]{:S(2)}) async-start(bf16[64,4,3584]{2,1,0:T(4,128)(2,1)} %reshape.126), calls=%async_computation.1 | async-start | bytes 3670016 | tf_op jit(solution)/shard_map/all_to_all | solution.py:93
  279.9 86.4 %copy-start.28 = (s32[128]{0:T(128)S(1)}, s32[128]{0:T(128)}, u32[]{:S(2)}) copy-start(s32[128]{0:T(128)} %copy-done.27) | copy-start | bytes 1540
  279.9 89.0 %copy-start.2 = (bf16[64,3584]{1,0:T(8,128)(2,1)S(1)}, bf16[64,3584]{1,0:T(8,128)(2,1)}, u32[]{:S(2)}) copy-start(bf16[64,3584]{1,0:T(8,128)(2,1)} %param.20) | copy-start | bytes 1376260
  352.4 309.7 %all-to-all-start.3 = ((bf16[64,4,3584]{2,1,0:T(4,128)(2,1)}), bf16[64,4,3584]{2,1,0:T(4,128)(2,1)}, u32[]{:S(2)}, u32[]{:S(2)}) async-start(bf16[64,4,3584]{2,1,0:T(4,128)(2,1)} %reshape.130), calls=%async_computation.3 | async-start | bytes 3670016 | tf_op jit(solution)/shard_map/all_to_all | solution.py:100
  366.3 275.4 %copy-start.18 = (s32[16,8]{1,0:T(8,128)S(1)}, s32[16,8]{1,0:T(8,128)}, u32[]{:S(2)}) copy-start(s32[16,8]{1,0:T(8,128)} %copy-done.17) | copy-start | bytes 1540
  366.3 476.2 %all-reduce.3.cloned.1.call-start = ((), (), s32[]{:S(2)}) async-start(), calls=%async_computation.7 | async-start | bytes 458752 | tf_op jit(solution)/shard_map/psum | solution.py:131
  369.2 272.5 %copy-start.19 = (bf16[16,64]{1,0:T(8,128)(2,1)}, bf16[16,64]{1,0:T(8,128)(2,1)S(1)}, u32[]{:S(2)}) copy-start(bf16[16,64]{1,0:T(8,128)(2,1)S(1)} %get-tuple-element.16) | copy-start | bytes 6148
  369.2 272.5 %copy-start.21 = (bf16[16,64]{1,0:T(8,128)(2,1)}, bf16[16,64]{1,0:T(8,128)(2,1)S(1)}, u32[]{:S(2)}) copy-start(bf16[16,64]{1,0:T(8,128)(2,1)S(1)} %get-tuple-element.18) | copy-start | bytes 6148
  503.6 147.6 %copy-start.14 = (bf16[256,64]{0,1:T(8,128)(2,1)S(1)}, bf16[256,64]{0,1:T(8,128)(2,1)}, u32[]{:S(2)}) copy-start(bf16[256,64]{0,1:T(8,128)(2,1)} %copy-done.13) | copy-start | bytes 98308
  648.4 5.4 copy-start.12
  655.1 3.9 copy-start.24
  659.0 2.3 copy-start.22
  666.0 2.3 copy-start.5
  666.0 2.3 copy-start.7
  666.0 2.3 copy-start.20
  668.3 174.2 %copy-start.26 = (f32[16]{0:T(128)S(1)}, f32[16]{0:T(128)}, u32[]{:S(2)}) copy-start(f32[16]{0:T(128)} %copy-done.25) | copy-start | bytes 196
  842.5 17.7 %copy-start.10 = (bf16[16,3584]{1,0:T(8,128)(2,1)S(1)}, bf16[16,3584]{1,0:T(8,128)(2,1)}, u32[]{:S(2)}) copy-start(bf16[16,3584]{1,0:T(8,128)(2,1)} %get-tuple-element.10) | copy-start | bytes 344068
  842.5 33.1 %copy-start.16 = (bf16[16,3584]{1,0:T(8,128)(2,1)S(1)}, bf16[16,3584]{1,0:T(8,128)(2,1)}, u32[]{:S(2)}) copy-start(bf16[16,3584]{1,0:T(8,128)(2,1)} %get-tuple-element.19) | copy-start | bytes 344068
  845.3 29.3 %all-to-all-start.4 = ((bf16[64,2,448]{2,1,0:T(2,128)(2,1)}), bf16[64,2,448]{2,1,0:T(2,128)(2,1)S(1)}, u32[]{:S(2)}, u32[]{:S(2)}) async-start(bf16[64,2,448]{2,1,0:T(2,128)(2,1)} %reshape.136), calls=%async_computation.4 | async-start | bytes 262144 | tf_op jit(solution)/shard_map/all_to_all | solution.py:149
Sparse Core Ops, SparseCore 0:
  669.3 173.1 all-reduce.2
where the time goes:
time: 886 us; the launch traced here: 883 us
  waiting for transfers between devices  424 us (48%)
  blocking collectives  272 us (31%)
  starting transfers between devices  94.6 us (11%)
  local copies, waits for them, and re-layouts  38.7 us (4%)
  matrix products  32.9 us (4%)
  between operations  14.4 us (2%)
    psum x1, waiting for transfers between devices, per_device(): lax.psum((routed_out + shared_out).astype(jnp.bfloat16), 'expert')  172 us
    all_gather x1, blocking collectives, per_device(): lax.all_gather(shared_gate_delta, 'replica', axis=0, tiled=True)  134 us
    all_to_all x1, waiting for transfers between devices, per_device(): lax.all_to_all(send_rows, 'replica', split_axis=0, concat_axis=0, tiled=T...  76.7 us
    all_to_all x1, waiting for transfers between devices, per_device(): lax.all_to_all(send_cots, 'replica', split_axis=0, concat_axis=0, tiled=T...  74.8 us
    all_to_all x1, waiting for transfers between devices, per_device(): lax.all_to_all(part_out.reshape(groups, capacity, model_width), 'replica'...  72.5 us
    all_gather x1, blocking collectives, per_device(): lax.all_gather(shared_act, 'replica', axis=0, tiled=True)  69.7 us
    all_gather x1, blocking collectives, per_device(): lax.all_gather(shared_up_delta, 'replica', axis=0, tiled=True)  68.4 us
    all_to_all x1, starting transfers between devices, per_device(): lax.all_to_all(send_cots, 'replica', split_axis=0, concat_axis=0, tiled=T...  22.9 us
  transfers between devices with their start and end apart: 8, of which 7 were waited for; matrix products, arithmetic and copies ran while one was open for 6% of the time, Pallas kernels for 0%

commit v1 on v0

v1 whole, which is shorter than its diff:
```python
import jax
import jax.numpy as jnp
from jax import lax
from jax.experimental import pallas as pl
from jax.experimental.pallas import tpu as pltpu
from jax.sharding import PartitionSpec as P

F32, BF16 = jnp.float32, jnp.bfloat16
MESH = pl.DeviceIdType.MESH
LANE = 128
WIDTH, UNITS, TOK, FAN = 3584, 64, 16, 8
RING, PEERS, SLOTS = 8, 64, 4
QUARTER = WIDTH // 4
TILES = QUARTER // LANE
HALF_ROWS = PEERS * SLOTS // 2
UNIT_ROWS = HALF_ROWS + TOK
SPLIT = 64
COLS = WIDTH // PEERS
PACK = 384


def iota(shape, axis):
    return lax.broadcasted_iota(jnp.int32, shape, axis)


def mul(left, right):
    return jnp.dot(left, right, preferred_element_type=F32)


def mul_nt(left, right):
    return lax.dot_general(left, right, (((1,), (1,)), ((), ())), preferred_element_type=F32)


def mul_tn(left, right):
    return lax.dot_general(left, right, (((0,), (0,)), ((), ())), preferred_element_type=F32)


def silu_slope(values, sig):
    return sig * (1.0 + values * (1.0 - sig))


def sigmoid(values):
    return 1.0 / (1.0 + jnp.exp(-values))


def feature_tile(f, j):
    return slice(f * QUARTER + j * LANE, f * QUARTER + (j + 1) * LANE)


def features(f):
    return slice(f * QUARTER, (f + 1) * QUARTER)


def layer_kernel(
    ids_ref, scores_ref, hidden_ref, gain_ref, grad_ref,
    wg_hbm, wu_hbm, wd_hbm, sg_hbm, su_hbm, sd_hbm,
    moe_ref, hidden_grad_ref, gain_grad_ref, gg_ref, ug_ref, dg_ref, shared_ref,
    wg, wu, wd, sg, su, sd, load_sem,
    normed_ref, normalized_ref,
    place_hi_ref, place_lo_ref,
    send1, recv1, units, parts, sibs,
    ring_up, ring_dn, got_up, got_dn, final_ref,
    side_send, side_recv, send2, recv2,
    tok_ref, tok_sib, full_ref, gain_send, gain_recv,
    s1_s, s1_r, side_s, side_r, s2_s, s2_r, g_s, g_r,
    up_s, up_r, dn_s, dn_r, hand_s, hand_r, sib_s, sib_r,
    rup_s, rup_r, rdn_s, rdn_r, t_s, t_r, e_s, e_r,
):
    expert = lax.axis_index("expert")
    me = lax.axis_index("replica")
    y, core = expert // 2, expert % 2
    quarter = y % 4
    is_rows = y < 4
    sibling = expert + 1 - 2 * core
    up = ((y + 1) % RING) * 2 + core
    down = ((y + RING - 1) % RING) * 2 + core

    def at_replica(peer):
        return (expert, peer)

    def at_expert(other):
        return (other, me)

    def remote(src, dst, send, recv, device):
        return pltpu.make_async_remote_copy(
            src_ref=src, dst_ref=dst, send_sem=send, recv_sem=recv, device_id=device, device_id_type=MESH
        )

    barrier = pltpu.get_barrier_semaphore()

    def greet_replica(k, carry):
        pl.semaphore_signal(barrier, inc=1, device_id=at_replica((me + k) % PEERS), device_id_type=MESH)
        return carry

    def greet_chip(k, carry):
        pl.semaphore_signal(
            barrier, inc=1, device_id=at_expert(((y + k) % RING) * 2 + core), device_id_type=MESH
        )
        return carry

    lax.fori_loop(1, PEERS, greet_replica, 0)
    lax.fori_loop(1, RING, greet_chip, 0)
    pl.semaphore_signal(barrier, inc=1, device_id=at_expert(sibling), device_id_type=MESH)

    loads = []
    for n, (src, dst) in enumerate(((sg_hbm, sg), (su_hbm, su), (sd_hbm, sd), (wg_hbm, wg), (wu_hbm, wu), (wd_hbm, wd))):
        loads.append(pltpu.make_async_copy(src, dst, load_sem.at[n]))
        loads[-1].start()

    widened = hidden_ref[...].astype(F32)
    inv_rms = lax.rsqrt(jnp.mean(widened * widened, axis=-1, keepdims=True) + 1e-06)
    normalized = widened * inv_rms
    normalized_ref[...] = normalized
    normed_ref[...] = (normalized * gain_ref[...]).astype(BF16)

    scores = scores_ref[...]
    weights = 2.5 * scores / jnp.sum(scores, axis=0, keepdims=True)
    expert_row = iota((PEERS, TOK), 0)
    member = jnp.zeros((PEERS, TOK), F32)
    gate = jnp.zeros((PEERS, TOK), F32)
    for k in range(FAN):
        hit = expert_row == ids_ref[k : k + 1, :]
        member = member + jnp.where(hit, 1.0, 0.0)
        gate = gate + jnp.where(hit, weights[k : k + 1, :], 0.0)
    before = jnp.where(iota((TOK, TOK), 0) < iota((TOK, TOK), 1), 1.0, 0.0).astype(BF16)
    rank = mul(member.astype(BF16), before)
    code = jnp.where(member > 0.5, rank, -1.0).astype(BF16)
    gate_hi = gate.astype(BF16)
    gate_lo = (gate - gate_hi.astype(F32)).astype(BF16)

    wide = TILES * TOK
    rows = PEERS * 16
    spread = jnp.where(iota((rows, PEERS), 0) // 16 == iota((rows, PEERS), 1), 1.0, 0.0).astype(BF16)
    tile = jnp.where(iota((TOK, wide), 1) % TOK == iota((TOK, wide), 0), 1.0, 0.0).astype(BF16)

    def expand(small):
        return mul(spread, mul(small, tile).astype(BF16))

    row_at, col_at = iota((rows, wide), 0), iota((rows, wide), 1)
    slot_of = (2 * core + row_at % 2).astype(F32)
    chosen = (expand(code) == slot_of) & ((row_at % 16) // 2 == col_at // TOK)
    onehot = jnp.where(chosen, 1.0, 0.0)
    hi_full = onehot * expand(gate_hi)
    lo_full = onehot * expand(gate_lo)
    place = onehot.astype(BF16)
    place_hi_ref[...] = jnp.where(is_rows, hi_full, onehot).astype(BF16)
    place_lo_ref[...] = jnp.where(is_rows, lo_full, 0.0).astype(BF16)
    row_scale = jnp.where(is_rows, 1.0, jnp.sum(hi_full + lo_full, axis=1, keepdims=True))

    mine = pl.ds(pl.multiple_of(quarter * QUARTER, LANE), QUARTER)
    source = jnp.where(is_rows, normed_ref[:, mine], grad_ref[:, mine])
    stacked = jnp.concatenate([source[:, j * LANE : (j + 1) * LANE] for j in range(TILES)], axis=0)
    outgoing = (mul(place, stacked) * row_scale).astype(BF16)
    send1[...] = outgoing.reshape(PEERS, 16, LANE)
    recv1[pl.ds(me, 1)] = send1[pl.ds(me, 1)]

    pl.semaphore_wait(barrier, PEERS - 1 + RING - 1 + 1)

    def exchange(src, dst, sends, recvs):
        def start(k, carry):
            peer = (me + k) % PEERS
            remote(src.at[peer], dst.at[me], sends.at[peer], recvs.at[me], at_replica(peer)).start()
            return carry

        lax.fori_loop(1, PEERS, start, 0)

    def arrived(dst, recvs, sends):
        def wait(k, carry):
            peer = (me + k) % PEERS
            remote(dst.at[peer], dst.at[peer], sends.at[peer], recvs.at[peer], at_replica(peer)).wait_recv()
            return carry

        lax.fori_loop(1, PEERS, wait, 0)

    def sent(src, sends, recvs):
        def wait(k, carry):
            peer = (me + k) % PEERS
            remote(src.at[peer], src.at[peer], sends.at[peer], recvs.at[peer], at_replica(peer)).wait_send()
            return carry

        lax.fori_loop(1, PEERS, wait, 0)

    exchange(send1, recv1, s1_s, s1_r)

    for load in loads[:3]:
        load.wait()
    normed = normed_ref[...]
    shared_pre = mul_nt(normed, sg[...])
    shared_up = mul_nt(normed, su[...])
    shared_sig = sigmoid(shared_pre)
    shared_silu = shared_pre * shared_sig
    shared_act = (shared_silu * shared_up).astype(BF16)
    shared_act_grad = mul_nt(grad_ref[...], sd[...])
    shared_gate_delta = (shared_act_grad * shared_up * silu_slope(shared_pre, shared_sig)).astype(BF16)
    shared_up_delta = (shared_act_grad * shared_silu).astype(BF16)
    for f in range(4):
        parts[f, 0, HALF_ROWS:, :] = mul(shared_act, sd[:, features(f)]).astype(BF16)
        parts[4 + f, 0, HALF_ROWS:, :] = (
            mul(shared_gate_delta, sg[:, features(f)]) + mul(shared_up_delta, su[:, features(f)])
        ).astype(BF16)
        parts[f, 1, HALF_ROWS:, :] = jnp.zeros((TOK, QUARTER), BF16)
        parts[4 + f, 1, HALF_ROWS:, :] = jnp.zeros((TOK, QUARTER), BF16)

    deltas = jnp.concatenate(
        [shared_gate_delta, shared_up_delta, shared_act, jnp.zeros((TOK, UNITS), BF16)], axis=1
    )
    side_send[:, :, LANE:] = jnp.broadcast_to(deltas[None], (PEERS, TOK, 2 * LANE))
    for m in range(16):
        first = min(m * COLS // LANE, TILES - 2)
        offset = m * COLS - first * LANE
        window = slice(first * LANE, (first + 2) * LANE)
        both = jnp.concatenate(
            [
                jnp.concatenate([ref[:, features(f)][:, window] for f in range(4)], axis=0)
                for ref in (normed_ref, grad_ref)
            ],
            axis=1,
        )
        at, lane = iota((4 * LANE, LANE), 0), iota((4 * LANE, LANE), 1)
        from_row = (at < 2 * LANE) & (at - offset == lane) & (lane < COLS)
        from_grad = (at >= 2 * LANE) & (at - 2 * LANE - offset == lane - COLS) & (lane >= COLS) & (lane < 2 * COLS)
        moved = mul(both, jnp.where(from_row | from_grad, 1.0, 0.0).astype(BF16)).astype(BF16)
        for f in range(4):
            side_send[16 * f + m, :, :LANE] = moved[f * TOK : (f + 1) * TOK]
    side_recv[pl.ds(me, 1)] = side_send[pl.ds(me, 1)]

    def unit_to_message(shape, unit_axis):
        at = iota(shape, unit_axis)
        lane = at % LANE
        message = (lane // 2) * 16 + (at // LANE) * 2 + lane % 2
        return jnp.where(message == iota(shape, 1 - unit_axis), 1.0, 0.0).astype(BF16)

    pick = unit_to_message((TILES * HALF_ROWS, rows), 0)
    arrived(recv1, s1_r, s1_s)
    gathered = mul(pick, recv1[...].reshape(rows, LANE)).astype(BF16)
    for j in range(TILES):
        units[y, core, :, j * LANE : (j + 1) * LANE] = gathered[j * HALF_ROWS : (j + 1) * HALF_ROWS]

    exchange(side_send, side_recv, side_s, side_r)

    def unit(chip, lo=0, hi=HALF_ROWS):
        return units.at[chip, core, lo:hi]

    def ring_copy(step, way):
        chip = (y + RING - step) % RING if way == 0 else (y + step) % RING
        lo, hi = (0, HALF_ROWS) if step < 3 else ((0, SPLIT) if way == 0 else (SPLIT, HALF_ROWS))
        sends, recvs, device = ((up_s, up_r, up), (dn_s, dn_r, down))[way]
        ref = unit(chip, lo, hi)
        return remote(ref, ref, sends.at[step], recvs.at[step], at_expert(device))

    def ring_arrival(step, way):
        chip = (y + RING - 1 - step) % RING if way == 0 else (y + 1 + step) % RING
        lo, hi = (0, HALF_ROWS) if step < 3 else ((0, SPLIT) if way == 0 else (SPLIT, HALF_ROWS))
        sends, recvs, device = ((up_s, up_r, up), (dn_s, dn_r, down))[way]
        ref = unit(chip, lo, hi)
        return ref, remote(ref, ref, sends.at[step], recvs.at[step], at_expert(device))

    def hand_over(n, ref):
        return remote(ref, ref, hand_s.at[n], hand_r.at[n], at_expert(sibling))

    def hand_arrival(n, chip, lo, hi):
        ref = units.at[chip, 1 - core, lo:hi]
        return remote(ref, ref, hand_s.at[n], hand_r.at[n], at_expert(sibling))

    waits = []
    for way in (0, 1):
        copy = ring_copy(0, way)
        copy.start()
        waits.append(copy)
    copy = hand_over(0, unit(y))
    copy.start()
    waits.append(copy)
    hands = [hand_arrival(0, y, 0, HALF_ROWS)]
    for step in range(4):
        for way in (0, 1):
            ref, arrival = ring_arrival(step, way)
            arrival.wait_recv()
            if step < 3:
                copy = ring_copy(step + 1, way)
                copy.start()
                waits.append(copy)
            number = 1 + 2 * step + way
            copy = hand_over(number, ref)
            copy.start()
            waits.append(copy)
            chip = (y + RING - 1 - step) % RING if way == 0 else (y + 1 + step) % RING
            lo, hi = (0, HALF_ROWS) if step < 3 else ((0, SPLIT) if way == 0 else (SPLIT, HALF_ROWS))
            hands.append(hand_arrival(number, chip, lo, hi))
    for load in loads[3:]:
        load.wait()
    for hand in hands:
        hand.wait_recv()

    def unit_rows(chip):
        return units[chip].reshape(2 * HALF_ROWS, QUARTER)

    pre_gate = sum(mul_nt(unit_rows(f), wg[:, features(f)]) for f in range(4))
    pre_up = sum(mul_nt(unit_rows(f), wu[:, features(f)]) for f in range(4))
    act_grad = sum(mul_nt(unit_rows(4 + f), wd[:, features(f)]) for f in range(4))
    sig = sigmoid(pre_gate)
    silu = pre_gate * sig
    activation = (silu * pre_up).astype(BF16)
    gate_delta = (act_grad * pre_up * silu_slope(pre_gate, sig)).astype(BF16)
    up_delta = (act_grad * silu).astype(BF16)
    for f in range(4):
        out_part = mul(activation, wd[:, features(f)]).astype(BF16)
        parts[f, :, :HALF_ROWS, :] = out_part.reshape(2, HALF_ROWS, QUARTER)
        in_part = (mul(gate_delta, wg[:, features(f)]) + mul(up_delta, wu[:, features(f)])).astype(BF16)
        parts[4 + f, :, :HALF_ROWS, :] = in_part.reshape(2, HALF_ROWS, QUARTER)

    order = (4, 3, 5, 2, 6, 1, 7, 0)
    for n, off in enumerate(order):
        chip = (y + off) % RING
        copy = remote(
            parts.at[chip, 1 - core], sibs.at[chip], sib_s.at[n], sib_r.at[n], at_expert(sibling)
        )
        copy.start()
        waits.append(copy)

    def pair_sum(off):
        chip = (y + off) % RING
        n = order.index(off)
        remote(sibs.at[chip], sibs.at[chip], sib_s.at[n], sib_r.at[n], at_expert(sibling)).wait_recv()
        return parts[chip, core].astype(F32) + sibs[chip].astype(F32)

    far = pair_sum(4).astype(BF16)
    ring_up[0, :SPLIT] = far[:SPLIT]
    ring_dn[0, SPLIT:] = far[SPLIT:]

    def reduce_copy(step, way):
        lo, hi = (0, UNIT_ROWS) if step else ((0, SPLIT) if way == 0 else (SPLIT, UNIT_ROWS))
        src, dst = ((ring_up, got_up), (ring_dn, got_dn))[way]
        sends, recvs, device = ((rup_s, rup_r, up), (rdn_s, rdn_r, down))[way]
        return remote(
            src.at[step, lo:hi], dst.at[step, lo:hi], sends.at[step], recvs.at[step], at_expert(device)
        )

    for way in (0, 1):
        copy = reduce_copy(0, way)
        copy.start()
        waits.append(copy)
    for step in range(1, 4):
        for way in (0, 1):
            total = pair_sum(4 - step if way == 0 else 4 + step)
            mine_ref, got = ((ring_up, got_up), (ring_dn, got_dn))[way]
            reduce_copy(step - 1, way).wait_recv()
            if step > 1:
                mine_ref[step] = (total + got[step - 1].astype(F32)).astype(BF16)
            elif way == 0:
                mine_ref[step, :SPLIT] = (total[:SPLIT] + got[0, :SPLIT].astype(F32)).astype(BF16)
                mine_ref[step, SPLIT:] = total[SPLIT:].astype(BF16)
            else:
                mine_ref[step, :SPLIT] = total[:SPLIT].astype(BF16)
                mine_ref[step, SPLIT:] = (total[SPLIT:] + got[0, SPLIT:].astype(F32)).astype(BF16)
            copy = reduce_copy(step, way)
            copy.start()
            waits.append(copy)
    for f in range(4):
        row_block, cot_block = unit_rows(f), unit_rows(4 + f)
        gg_ref[:, features(f)] = mul_tn(gate_delta, row_block).astype(BF16)
        ug_ref[:, features(f)] = mul_tn(up_delta, row_block).astype(BF16)
        dg_ref[:, features(f)] = mul_tn(activation, cot_block).astype(BF16)
    own = pair_sum(0)
    for way in (0, 1):
        reduce_copy(3, way).wait_recv()
    final_ref[...] = own + got_up[3].astype(F32) + got_dn[3].astype(F32)

    finished = jnp.concatenate(
        [final_ref[:HALF_ROWS, j * LANE : (j + 1) * LANE].astype(BF16) for j in range(TILES)], axis=0
    )
    spill = unit_to_message((rows, TILES * HALF_ROWS), 1)
    send2[...] = mul(spill, finished).astype(BF16).reshape(PEERS, 16, LANE)
    recv2[pl.ds(me, 1)] = send2[pl.ds(me, 1)]
    exchange(send2, recv2, s2_s, s2_r)

    arrived(side_recv, side_r, side_s)
    every = side_recv[...].reshape(PEERS * TOK, PACK)
    shared_ref[...] = mul_tn(every[:, LANE:], every[:, :LANE]).astype(BF16)

    arrived(recv2, s2_r, s2_s)
    returned = recv2[...].reshape(rows, LANE)
    tokens = mul_tn(place_hi_ref[...], returned) + mul_tn(place_lo_ref[...], returned)
    shared_rows = jnp.concatenate(
        [final_ref[HALF_ROWS:, j * LANE : (j + 1) * LANE] for j in range(TILES)], axis=0
    )
    tok_ref[...] = tokens + shared_rows
    copy = remote(tok_ref, tok_sib, t_s, t_r, at_expert(sibling))
    copy.start()
    waits.append(copy)
    copy.wait_recv()
    full_ref[y] = (tok_ref[...] + tok_sib[...]).astype(BF16)

    def send_full(k, carry):
        chip = (y + k) % RING
        remote(full_ref.at[y], full_ref.at[y], e_s.at[k], e_r.at[k], at_expert(chip * 2 + core)).start()
        return carry

    def wait_full(k, carry):
        chip = (y + RING - k) % RING
        remote(full_ref.at[chip], full_ref.at[chip], e_s.at[k], e_r.at[k], at_expert(chip * 2 + core)).wait_recv()
        return carry

    def wait_full_sent(k, carry):
        remote(full_ref.at[y], full_ref.at[y], e_s.at[k], e_r.at[k], at_expert(up)).wait_send()
        return carry

    lax.fori_loop(1, RING, send_full, 0)
    lax.fori_loop(1, RING, wait_full, 0)

    def grad_tile(f, j):
        return full_ref[4 + f, j * TOK : (j + 1) * TOK, :].astype(F32)

    inner = jnp.zeros((TOK, 1), F32)
    for f in range(4):
        terms = []
        for j in range(TILES):
            at = feature_tile(f, j)
            term = grad_tile(f, j) * normalized_ref[:, at]
            terms.append(jnp.sum(term, axis=0, keepdims=True))
            inner = inner + jnp.sum(term * gain_ref[:, at], axis=1, keepdims=True)
        terms.append(jnp.zeros((1, LANE), F32))
        line = jnp.concatenate(terms, axis=1)
        for m in range(16):
            gain_send[16 * f + m] = line[:, m * COLS : m * COLS + LANE]
    gain_recv[pl.ds(me, 1)] = gain_send[pl.ds(me, 1)]
    exchange(gain_send, gain_recv, g_s, g_r)
    inner = inner * (1.0 / WIDTH)
    inv_again = lax.rsqrt(
        jnp.mean(jnp.square(hidden_ref[...].astype(F32)), axis=-1, keepdims=True) + 1e-06
    )
    for f in range(4):
        for j in range(TILES):
            at = feature_tile(f, j)
            moe_ref[:, at] = full_ref[f, j * TOK : (j + 1) * TOK, :]
            scaled = grad_tile(f, j) * gain_ref[:, at]
            hidden_grad_ref[:, at] = (inv_again * (scaled - normalized_ref[:, at] * inner)).astype(BF16)

    for copy in waits:
        copy.wait_send()
    lax.fori_loop(1, RING, wait_full_sent, 0)
    sent(send1, s1_s, s1_r)
    sent(side_send, side_s, side_r)
    sent(send2, s2_s, s2_r)
    sent(gain_send, g_s, g_r)
    arrived(gain_recv, g_r, g_s)
    gain_grad_ref[...] = jnp.sum(gain_recv[...], axis=0)


def per_device(
    hidden_in, norm_gain, expert_ids, gate_scores, w_gate, w_up, w_down, shared_gate, shared_up, shared_down, out_grad
):
    vmem, hbm = pl.BlockSpec(memory_space=pltpu.VMEM), pl.BlockSpec(memory_space=pl.ANY)
    dma = pltpu.SemaphoreType.DMA
    matrix = (UNITS, WIDTH)
    message = (PEERS, 16, LANE)
    outs = pl.pallas_call(
        layer_kernel,
        out_shape=(
            jax.ShapeDtypeStruct((TOK, WIDTH), BF16),
            jax.ShapeDtypeStruct((TOK, WIDTH), BF16),
            jax.ShapeDtypeStruct((1, LANE), F32),
            jax.ShapeDtypeStruct(matrix, BF16),
            jax.ShapeDtypeStruct(matrix, BF16),
            jax.ShapeDtypeStruct(matrix, BF16),
            jax.ShapeDtypeStruct((2 * LANE, LANE), BF16),
        ),
        in_specs=[vmem] * 5 + [hbm] * 6,
        out_specs=[vmem] * 7,
        scratch_shapes=[pltpu.VMEM(matrix, BF16)] * 6
        + [
            dma((6,)),
            pltpu.VMEM((TOK, WIDTH), BF16),
            pltpu.VMEM((TOK, WIDTH), F32),
            pltpu.VMEM((PEERS * 16, TILES * TOK), BF16),
            pltpu.VMEM((PEERS * 16, TILES * TOK), BF16),
            pltpu.VMEM(message, BF16),
            pltpu.VMEM(message, BF16),
            pltpu.VMEM((RING, 2, HALF_ROWS, QUARTER), BF16),
            pltpu.VMEM((RING, 2, UNIT_ROWS, QUARTER), BF16),
            pltpu.VMEM((RING, UNIT_ROWS, QUARTER), BF16),
        ]
        + [pltpu.VMEM((4, UNIT_ROWS, QUARTER), BF16)] * 4
        + [
            pltpu.VMEM((UNIT_ROWS, QUARTER), F32),
            pltpu.VMEM((PEERS, TOK, PACK), BF16),
            pltpu.VMEM((PEERS, TOK, PACK), BF16),
            pltpu.VMEM(message, BF16),
            pltpu.VMEM(message, BF16),
            pltpu.VMEM((TILES * TOK, LANE), F32),
            pltpu.VMEM((TILES * TOK, LANE), F32),
            pltpu.VMEM((RING, TILES * TOK, LANE), BF16),
            pltpu.VMEM((PEERS, 1, LANE), F32),
            pltpu.VMEM((PEERS, 1, LANE), F32),
        ]
        + [dma((PEERS,))] * 8
        + [dma((4,))] * 4
        + [dma((9,))] * 2
        + [dma((RING,))] * 2
        + [dma((4,))] * 4
        + [dma] * 2
        + [dma((RING,))] * 2,
        compiler_params=pltpu.CompilerParams(
            collective_id=0, has_side_effects=True, vmem_limit_bytes=56 * 1024 * 1024
        ),
    )(
        expert_ids.T,
        gate_scores.astype(F32).T,
        hidden_in,
        norm_gain.reshape(1, WIDTH),
        out_grad,
        w_gate[0],
        w_up[0],
        w_down[0],
        shared_gate,
        shared_up,
        shared_down,
    )
    moe_out, hidden_grad, gain_grad, gate_grad, up_grad, down_grad, shared = outs
    return (
        moe_out,
        hidden_grad,
        gain_grad[0, :COLS],
        gate_grad[None],
        up_grad[None],
        down_grad[None],
        shared[:UNITS, :COLS],
        shared[UNITS : 2 * UNITS, :COLS],
        shared[2 * UNITS : 3 * UNITS, COLS : 2 * COLS],
    )


def solution(mesh):
    rows, weights, shared = P("replica", None), P("replica", "expert", None), P("expert", None)
    return jax.shard_map(
        per_device,
        mesh=mesh,
        in_specs=(rows, P(), rows, rows, weights, weights, weights, shared, shared, shared, rows),
        out_specs=(rows, rows, P("replica"), weights, weights, weights) + (P("expert", "replica"),) * 3,
        check_vma=False,
    )
```

time: 886 us -> 152 us (0.17)
  waiting for transfers between devices: 424 us -> 0 us
  blocking collectives: 272 us -> 0 us
  Pallas kernels: 0 us -> 137 us
  starting transfers between devices: 94.6 us -> 0 us
  matrix products: 32.9 us -> 0 us
  local copies, waits for them, and re-layouts: 38.7 us -> 12.3 us
  between operations: 14.4 us -> 0.67 us
    all_gather x3 -> x0, blocking collectives: 272 us -> none  [the longest x1 134 us: per_device(): lax.all_gather(shared_gate_delta, 'replica', axis=0, tiled=True)]
    all_to_all x7 -> x0, waiting for transfers between devices: 252 us -> none  [the longest x1 76.7 us: per_device(): lax.all_to_all(send_rows, 'replica', split_axis=0, concat_axis=0, tiled=T...]
    psum x1 -> x0, waiting for transfers between devices: 172 us -> none  [per_device(): lax.psum((routed_out + shared_out).astype(jnp.bfloat16), 'expert')]
    pallas_call x0 -> x1, Pallas kernels: none -> 137 us  [per_device(): pl.pallas_call(layer_kernel, out_shape=(jax.ShapeDtypeStruct((TOK, WIDTH)...]
    all_to_all x7 -> x0, starting transfers between devices: 94.6 us -> none  [the longest x1 22.9 us: per_device(): lax.all_to_all(send_cots, 'replica', split_axis=0, concat_axis=0, tiled=T...]
    dot_general x22 -> x0, matrix products: 32.9 us -> none  [the longest x8 12.4 us: inner_rows(): lax.dot_general(left, right, (((0,), (0,)), ((), ())), preferred_element_...]
    reshape x8 -> x1, local copies, waits for them, and re-layouts: 26 us -> 1.33 us  [per_device(): norm_gain.reshape(1, WIDTH)]
  transfers between devices with their start and end apart: 8 -> 0, of which waited for: 7 -> 0; matrix products, arithmetic and copies ran while one was open for 6% -> 0% of each run, Pallas kernels for 0% -> 0%
where the time goes in v1:
time: 152 us; the launch traced here: 151 us
  Pallas kernels  137 us (90%)
  local copies, waits for them, and re-layouts  12.3 us (8%)
    pallas_call x1, Pallas kernels, per_device(): pl.pallas_call(layer_kernel, out_shape=(jax.ShapeDtypeStruct((TOK, WIDTH)...  137 us
    unnamed x16, local copies, waits for them, and re-layouts  8.99 us

profile of v1, /device:TPU:1, one launch (start us, length us, event | category | flops | bytes accessed | tf_op | source)
XLA Modules:
  0.0 150.9 jit_solution(15067575862378201396)
XLA Ops:
  0.6 0.0 copy-start.3
  0.7 0.7 copy-done.3
  1.3 0.6 convert_bitcast_fusion.scores_ref
  1.9 1.3 reshape.21.gain_ref
  3.3 137.3 %shard_map.178 = (bf16[16,3584]{1,0:T(8,128)(2,1)}, bf16[16,3584]{1,0:T(8,128)(2,1)}, f32[1,128]{1,0:T(1,128)}, bf16[64,3584]{1,0:T(8,128)(2,1)}, bf16[64,3584]{...) custom-call(s32[8,16]{1,0:T(8,128)} %bitcast.17, f32[8,16]{1,0:T(8,128)} %convert_bitcast_fusion.scores_ref, ...), custom_call_target="tpu_custom_call" | custom-call | tf_op jit(solution)/shard_map/pallas_call | solution.py:456
  140.6 0.0 copy-start.2
  140.6 1.2 slice_bitcast_fusion
  141.8 0.8 fusion
  142.6 0.7 copy.22
  143.3 0.7 copy.21
  144.0 0.7 copy.20
  144.7 1.6 %copy.28 = bf16[16,3584]{1,0:T(8,128)(2,1)} copy(bf16[16,3584]{1,0:T(8,128)(2,1)} %get-tuple-element.44) | data formatting | bytes 229376
  146.2 1.6 %copy.29 = bf16[16,3584]{1,0:T(8,128)(2,1)} copy(bf16[16,3584]{1,0:T(8,128)(2,1)} %get-tuple-element.45) | data formatting | bytes 229376
  147.8 0.0 copy-done.2
  147.8 0.0 copy-start.1
  147.8 0.8 copy.30
  148.6 0.4 copy-done.1
  149.0 0.0 copy-start
  149.0 0.8 copy.31
  149.7 0.4 copy-done
  150.2 0.8 copy.32
Async XLA Ops:
  0.6 0.7 copy-start.3
  140.6 7.2 %copy-start.2 = (bf16[64,3584]{1,0:T(8,128)(2,1)S(1)}, bf16[64,3584]{1,0:T(8,128)(2,1)}, u32[]{:S(2)}) copy-start(bf16[64,3584]{1,0:T(8,128)(2,1)} %get-tuple-element.19) | copy-start | bytes 1376260
  147.8 1.2 copy-start.1
  149.0 1.2 copy-start

commit v2 on v1

v2 whole, which is shorter than its diff:
```python
import jax
import jax.numpy as jnp
from jax import lax
from jax.experimental import pallas as pl
from jax.experimental.pallas import tpu as pltpu
from jax.sharding import PartitionSpec as P

F32, BF16 = jnp.float32, jnp.bfloat16
MESH = pl.DeviceIdType.MESH
LANE = 128
WIDTH, UNITS, TOK, FAN = 3584, 64, 16, 8
RING, PEERS, SLOTS = 8, 64, 4
QUARTER = WIDTH // 4
TILES = QUARTER // LANE
HALF_ROWS = PEERS * SLOTS // 2
UNIT_ROWS = HALF_ROWS + TOK
PARTS = 2 * RING
HALF = PEERS // 2
SPAN = HALF_ROWS // 2
OWN = PEERS - 1
COLS = WIDTH // PEERS


def iota(shape, axis):
    return lax.broadcasted_iota(jnp.int32, shape, axis)


def mul(left, right):
    return jnp.dot(left, right, preferred_element_type=F32)


def mul_nt(left, right):
    return lax.dot_general(left, right, (((1,), (1,)), ((), ())), preferred_element_type=F32)


def mul_tn(left, right):
    return lax.dot_general(left, right, (((0,), (0,)), ((), ())), preferred_element_type=F32)


def silu_slope(values, sig):
    return sig * (1.0 + values * (1.0 - sig))


def sigmoid(values):
    return 1.0 / (1.0 + jnp.exp(-values))


def feature_tile(f, j):
    return slice(f * QUARTER + j * LANE, f * QUARTER + (j + 1) * LANE)


def features(f):
    return slice(f * QUARTER, (f + 1) * QUARTER)


def layer_kernel(
    ids_ref, scores_ref, hidden_ref, gain_ref, grad_ref,
    wg_hbm, wu_hbm, wd_hbm, sg_hbm, su_hbm, sd_hbm,
    moe_ref, hidden_grad_ref, gain_grad_ref, shared_gate_ref, shared_up_ref, shared_down_ref,
    gg_hbm, ug_hbm, dg_hbm,
    wg, wu, wd, sg, su, sd, load_sem,
    normed_ref, normalized_ref, back_hi_ref, back_lo_ref, pick_ref, spill_ref,
    send1, recv1, units, parts, sibs,
    ring_up, ring_dn, got_up, got_dn, final_ref,
    side_send, side_recv, side_sib, send2, recv2,
    tok_ref, tok_sib, full_ref, gain_send, gain_recv, gain_all,
    gg_ref, ug_ref, dg_ref, store_sem,
    s1_s, s1_r, side_s, side_r, s2_s, s2_r, g_s, g_r,
    up_s, up_r, dn_s, dn_r, rup_s, rup_r, rdn_s, rdn_r, hand_s, hand_r, sib_s, sib_r,
    e_s, e_r, gb_s, gb_r, pair_s, pair_r,
):
    expert = lax.axis_index("expert")
    me = lax.axis_index("replica")
    y, core = expert // 2, expert % 2
    x, z = me // 16, me % 16
    quarter = y % 4
    is_rows = y < 4
    sibling = expert + 1 - 2 * core

    def at_replica(peer):
        return (expert, peer)

    def at_expert(other):
        return (other, me)

    def remote(src, dst, send, recv, device):
        return pltpu.make_async_remote_copy(
            src_ref=src, dst_ref=dst, send_sem=send, recv_sem=recv, device_id=device, device_id_type=MESH
        )

    def along_z(n):
        t = 15 - n
        odd = t % 2
        return odd * ((t + 1) // 2) + (1 - odd) * (16 - t // 2)

    def along_x(c):
        return (c + 1) % 4

    barrier = pltpu.get_barrier_semaphore()

    def greet_replica(k, carry):
        pl.semaphore_signal(barrier, inc=1, device_id=at_replica((me + k) % PEERS), device_id_type=MESH)
        return carry

    def greet_expert(k, carry):
        pl.semaphore_signal(barrier, inc=1, device_id=at_expert((expert + k) % PARTS), device_id_type=MESH)
        return carry

    lax.fori_loop(1, PEERS, greet_replica, 0)
    lax.fori_loop(1, PARTS, greet_expert, 0)

    loads = []
    for n, (src, dst) in enumerate(
        ((sg_hbm, sg), (su_hbm, su), (sd_hbm, sd), (wg_hbm.at[0], wg), (wu_hbm.at[0], wu), (wd_hbm.at[0], wd))
    ):
        loads.append(pltpu.make_async_copy(src, dst, load_sem.at[n]))
        loads[-1].start()

    widened = hidden_ref[...].astype(F32)
    inv_rms = lax.rsqrt(jnp.mean(widened * widened, axis=-1, keepdims=True) + 1e-06)
    for n in range(4 * TILES):
        at = slice(n * LANE, (n + 1) * LANE)
        normalized = widened[:, at] * inv_rms
        normalized_ref[:, at] = normalized
        normed_ref[:, at] = (normalized * gain_ref[n : n + 1, :]).astype(BF16)

    scores = scores_ref[...].astype(F32)
    weights = 2.5 * scores / jnp.sum(scores, axis=0, keepdims=True)
    row_q = iota((PEERS, TOK), 0)
    expert_of = ((x + along_x(row_q % 4)) % 4) * 16 + (z + along_z(row_q // 4)) % 16
    member = jnp.zeros((PEERS, TOK), F32)
    gate = jnp.zeros((PEERS, TOK), F32)
    for k in range(FAN):
        hit = expert_of == ids_ref[k : k + 1, :]
        member = member + jnp.where(hit, 1.0, 0.0)
        gate = gate + jnp.where(hit, weights[k : k + 1, :], 0.0)
    before = jnp.where(iota((TOK, TOK), 0) < iota((TOK, TOK), 1), 1.0, 0.0).astype(BF16)
    rank = mul(member.astype(BF16), before)
    code = jnp.where(member > 0.5, rank - (2 * core).astype(F32), -32.0).astype(BF16)
    gate_hi = gate.astype(BF16).astype(F32)
    gate_lo = gate - gate_hi

    rows = PEERS * 16
    at_row, at_lane = iota((rows, LANE), 0), iota((rows, LANE), 1)
    belongs = (at_lane == at_row // 16) | (at_lane == PEERS + (at_row % 16) // 2)
    belongs = belongs | ((at_lane == PEERS + 8) & (at_row % 2 == 1))
    spread = jnp.where(belongs, 1.0, 0.0).astype(BF16)
    tile = jnp.where(iota((TOK, LANE), 1) % TOK == iota((TOK, LANE), 0), 1.0, 0.0).astype(BF16)
    low, lane = iota((PEERS, LANE), 0), iota((PEERS, LANE), 1)
    rest = jnp.where(low < 8, jnp.where((low == lane // TOK) & (low < TILES), 0.0, -64.0), 0.0)
    rest = jnp.where(low == 8, -1.0, rest)

    def expand(small, below):
        return mul(spread, jnp.concatenate([mul(small.astype(BF16), tile), below], axis=0).astype(BF16))

    nothing = jnp.zeros((PEERS, LANE), F32)
    widths = [mul(small.astype(BF16), tile) for small in (code, jnp.where(is_rows, member, gate_hi))]
    table = jnp.concatenate(
        [jnp.concatenate(widths, axis=1), jnp.concatenate([rest, nothing], axis=1)], axis=0
    )
    found = mul(spread, table.astype(BF16))
    chosen = found[:, :LANE] == 0.0
    place = jnp.where(chosen, found[:, LANE:], 0.0).astype(BF16)
    mine = pl.ds(pl.multiple_of(quarter * QUARTER, LANE), QUARTER)
    source = jnp.where(is_rows, normed_ref[:, mine], grad_ref[:, mine])
    stacked = jnp.concatenate(
        [source[:, j * LANE : (j + 1) * LANE] for j in range(TILES)] + [jnp.zeros((TOK, LANE), BF16)], axis=0
    )
    send1[...] = mul(place, stacked).astype(BF16).reshape(PEERS, 16, LANE)
    recv1[OWN] = send1[OWN]

    pl.semaphore_wait(barrier, PEERS - 1 + PARTS - 1)

    def exchange(src, dst, send, recv, lo, hi, back=False):
        planes = []
        for c in range(4):
            planes.append(lax.rem(x + (4 - along_x(c) if back else along_x(c)), 4) * 16)

        def some(n, count):
            shift = along_z(n)
            row = lax.rem(z + (16 - shift if back else shift) + 16, 16)
            for c in range(count):
                q = 4 * n + c
                remote(src.at[q], dst.at[q], send, recv, at_replica(planes[c] + row)).start()

        def step(n, carry):
            some(n, 4)
            return carry

        lax.fori_loop(lo // 4, min(hi, OWN) // 4, step, 0)
        if hi > OWN:
            some(OWN // 4, 3)

    def arrived(dst, send, recv, lo, hi):
        ref = dst.at[lo : min(hi, OWN)]
        remote(ref, ref, send, recv, at_replica((me + 1) % PEERS)).wait_recv()

    def sent(src, send, recv):
        ref = src.at[:OWN]
        remote(ref, ref, send, recv, at_replica((me + 1) % PEERS)).wait_send()

    exchange(send1, recv1, s1_s, s1_r.at[0], HALF, PEERS)
    exchange(send1, recv1, s1_s, s1_r.at[1], 0, HALF)

    for load in loads[:3]:
        load.wait()
    normed = normed_ref[...]
    shared_pre = mul_nt(normed, sg[...])
    shared_up = mul_nt(normed, su[...])
    shared_sig = sigmoid(shared_pre)
    shared_silu = shared_pre * shared_sig
    shared_act = (shared_silu * shared_up).astype(BF16)
    shared_act_grad = mul_nt(grad_ref[...], sd[...])
    shared_gate_delta = (shared_act_grad * shared_up * silu_slope(shared_pre, shared_sig)).astype(BF16)
    shared_up_delta = (shared_act_grad * shared_silu).astype(BF16)

    def unit_to_message(shape, unit_axis):
        at = iota(shape, unit_axis)
        row = at % SPAN
        message = (row // 2) * 16 + (at // SPAN) * 2 + row % 2
        return jnp.where(message == iota(shape, 1 - unit_axis), 1.0, 0.0).astype(BF16)

    pick_ref[...] = unit_to_message((TILES * SPAN, HALF * 16), 0)

    def unpack(chunk):
        q = 0 if chunk else HALF
        lo = 0 if chunk else SPAN
        arrived(recv1, s1_s, s1_r.at[chunk], q, q + HALF)
        gathered = mul(pick_ref[...], recv1[q : q + HALF].reshape(HALF * 16, LANE)).astype(BF16)
        for j in range(TILES):
            units[y, core, lo : lo + SPAN, j * LANE : (j + 1) * LANE] = gathered[j * SPAN : (j + 1) * SPAN]

    waits, hands = [], [[], []]

    def launch(copy):
        copy.start()
        waits.append(copy)

    def chip_at(way, distance):
        return (y + distance) % RING if way == 0 else (y + RING - distance) % RING

    def gather_rows(chunk, distance, way):
        lo = 0 if chunk else SPAN
        if distance < 4:
            return lo, lo + SPAN
        return (lo, lo + SPAN // 2) if way == 0 else (lo + SPAN // 2, lo + SPAN)

    def gather_copy(chunk, distance, way, chip, hops=1):
        lo, hi = gather_rows(chunk, distance, way)
        sends, recvs = ((up_s, up_r), (dn_s, dn_r))[way]
        ref = units.at[chip, core, lo:hi]
        n = chunk * 4 + distance - 1
        return remote(ref, ref, sends.at[n], recvs.at[n], at_expert(chip_at(way, hops) * 2 + core))

    def hand_over(chunk, n, chip, lo, hi):
        n = chunk * 9 + n
        ref = units.at[chip, core, lo:hi]
        launch(remote(ref, ref, hand_s.at[n], hand_r.at[n], at_expert(sibling)))
        ref = units.at[chip, 1 - core, lo:hi]
        hands[chunk].append(remote(ref, ref, hand_s.at[n], hand_r.at[n], at_expert(sibling)))

    def gather_begin(chunk):
        for distance in (2, 1):
            for way in (0, 1):
                launch(gather_copy(chunk, distance, way, y, distance))
        hand_over(chunk, 0, y, *gather_rows(chunk, 1, 0))

    def gather_arrival(chunk, distance, way):
        chip = chip_at(1 - way, distance)
        gather_copy(chunk, distance, way, chip).wait_recv()
        return chip

    def gather_middle(chunk):
        homes = []
        for way in (0, 1):
            chip = gather_arrival(chunk, 2, way)
            launch(gather_copy(chunk, 4, way, chip, 2))
            launch(gather_copy(chunk, 3, way, chip, 1))
            homes.append(chip)
        for way in (0, 1):
            hand_over(chunk, 3 + way, homes[way], *gather_rows(chunk, 2, way))
        for way in (0, 1):
            chip = gather_arrival(chunk, 1, way)
            hand_over(chunk, 1 + way, chip, *gather_rows(chunk, 1, way))

    def gather_end(chunk):
        for distance in (3, 4):
            for way in (0, 1):
                chip = gather_arrival(chunk, distance, way)
                hand_over(chunk, 2 * distance - 1 + way, chip, *gather_rows(chunk, distance, way))

    unpack(0)
    gather_begin(0)

    for f in range(4):
        parts[f, 0, HALF_ROWS:, :] = mul(shared_act, sd[:, features(f)]).astype(BF16)
        parts[4 + f, 0, HALF_ROWS:, :] = (
            mul(shared_gate_delta, sg[:, features(f)]) + mul(shared_up_delta, su[:, features(f)])
        ).astype(BF16)
        parts[f, 1, HALF_ROWS:, :] = jnp.zeros((TOK, QUARTER), BF16)
        parts[4 + f, 1, HALF_ROWS:, :] = jnp.zeros((TOK, QUARTER), BF16)


    act_wide = jnp.concatenate([shared_act.astype(F32), jnp.zeros((TOK, LANE - UNITS), F32)], axis=1)
    side_send[:, :, :LANE] = jnp.broadcast_to(
        jnp.concatenate([shared_gate_delta, shared_up_delta], axis=1)[None], (PEERS, TOK, LANE)
    )

    def side_columns(m):
        first = min(m * COLS // LANE, TILES - 2)
        offset = m * COLS - first * LANE
        window = slice(first * LANE, (first + 2) * LANE)
        block = jnp.concatenate(
            [
                jnp.where(core == 0, normed_ref[:, features(f)][:, window], grad_ref[:, features(f)][:, window])
                for f in range(4)
            ],
            axis=0,
        )
        at, to = iota((2 * LANE, LANE), 0), iota((2 * LANE, LANE), 1)
        moves = (at - offset == to - UNITS) & (to >= UNITS) & (to < UNITS + COLS)
        moved = mul(block, jnp.where(moves, 1.0, 0.0).astype(BF16))
        for f in range(4):
            ahead = (m + 16 - z) % 16
            place_z = jnp.where(ahead <= 8, 2 * ahead - jnp.where(ahead > 0, 1, 0), 32 - 2 * ahead)
            q = (15 - place_z) * 4 + (f + 7 - x) % 4
            side_send[q, :, LANE:] = (moved[f * TOK : (f + 1) * TOK] + act_wide).astype(BF16)

    for m in range(16):
        side_columns(m)
    gather_middle(0)
    side_recv[OWN] = side_send[OWN]

    spill_ref[...] = unit_to_message((HALF * 16, TILES * SPAN), 1)
    back_hi = jnp.where(chosen, expand(jnp.where(is_rows, gate_hi, member), nothing), 0.0)
    back_lo = jnp.where(chosen, expand(jnp.where(is_rows, gate_lo, 0.0), nothing), 0.0)
    back_hi_ref[...] = jnp.transpose(back_hi).astype(BF16)
    back_lo_ref[...] = jnp.transpose(back_lo).astype(BF16)

    def send_side(batch):
        exchange(side_send, side_recv, side_s, side_r, 16 * batch, 16 * batch + 16)

    unpack(1)
    gather_begin(1)
    send_side(0)
    gather_end(0)
    send_side(1)
    gather_middle(1)
    send_side(2)

    def unit_rows(chip, chunk):
        lo = 0 if chunk else SPAN
        return units[chip, :, lo : lo + SPAN, :].reshape(2 * SPAN, QUARTER)

    def run_expert(chunk):
        lo = 0 if chunk else SPAN
        for hand in hands[chunk]:
            hand.wait_recv()
        pre_gate = sum(mul_nt(unit_rows(f, chunk), wg[:, features(f)]) for f in range(4))
        pre_up = sum(mul_nt(unit_rows(f, chunk), wu[:, features(f)]) for f in range(4))
        act_grad = sum(mul_nt(unit_rows(4 + f, chunk), wd[:, features(f)]) for f in range(4))
        sig = sigmoid(pre_gate)
        silu = pre_gate * sig
        activation = (silu * pre_up).astype(BF16)
        gate_delta = (act_grad * pre_up * silu_slope(pre_gate, sig)).astype(BF16)
        up_delta = (act_grad * silu).astype(BF16)
        for f in range(4):
            out_part = mul(activation, wd[:, features(f)]).astype(BF16)
            parts[f, :, lo : lo + SPAN, :] = out_part.reshape(2, SPAN, QUARTER)
            in_part = (mul(gate_delta, wg[:, features(f)]) + mul(up_delta, wu[:, features(f)])).astype(BF16)
            parts[4 + f, :, lo : lo + SPAN, :] = in_part.reshape(2, SPAN, QUARTER)
        return activation, gate_delta, up_delta

    order = (4, 3, 5, 1, 7, 2, 6, 0)

    def reduce_rows(chunk):
        lo, hi = (0, SPAN) if chunk else (SPAN, UNIT_ROWS)
        return lo, lo + SPAN // 2, hi

    def pair_copy(chunk, n, chip):
        lo, _, hi = reduce_rows(chunk)
        n = chunk * 8 + n
        return remote(
            parts.at[chip, 1 - core, lo:hi], sibs.at[chip, lo:hi], sib_s.at[n], sib_r.at[n], at_expert(sibling)
        )

    def pair_begin(chunk):
        for n, off in enumerate(order):
            launch(pair_copy(chunk, n, (y + off) % RING))

    def pair_sum(chunk, off):
        lo, _, hi = reduce_rows(chunk)
        chip = (y + off) % RING
        pair_copy(chunk, order.index(off), chip).wait_recv()
        return parts[chip, core, lo:hi].astype(F32) + sibs[chip, lo:hi].astype(F32)

    slot_hops = (2, 1, 1, 2)

    def reduce_copy(chunk, slot, way):
        lo, mid, hi = reduce_rows(chunk)
        if slot == 0:
            lo, hi = (lo, mid) if way == 0 else (mid, hi)
        src, dst = ((ring_up, got_up), (ring_dn, got_dn))[way]
        sends, recvs = ((rup_s, rup_r), (rdn_s, rdn_r))[way]
        n = chunk * 4 + slot
        device = at_expert(chip_at(way, slot_hops[slot]) * 2 + core)
        return remote(src.at[slot, lo:hi], dst.at[slot, lo:hi], sends.at[n], recvs.at[n], device)

    def offset(way, distance):
        return distance if way == 0 else RING - distance

    def reduce_begin(chunk):
        lo, mid, hi = reduce_rows(chunk)
        far = pair_sum(chunk, 4).astype(BF16)
        ring_up[0, lo:mid] = far[: mid - lo]
        ring_dn[0, mid:hi] = far[mid - lo :]
        for way in (0, 1):
            launch(reduce_copy(chunk, 0, way))
        for slot, distance in ((1, 3), (2, 1)):
            for way in (0, 1):
                (ring_up, ring_dn)[way][slot, lo:hi] = pair_sum(chunk, offset(way, distance)).astype(BF16)
                launch(reduce_copy(chunk, slot, way))

    def reduce_middle(chunk):
        lo, mid, hi = reduce_rows(chunk)
        for way in (0, 1):
            total = pair_sum(chunk, offset(way, 2))
            out, got = ((ring_up, got_up), (ring_dn, got_dn))[way]
            reduce_copy(chunk, 1, way).wait_recv()
            total = total + got[1, lo:hi].astype(F32)
            reduce_copy(chunk, 0, way).wait_recv()
            half, rest_of = total[: mid - lo], total[mid - lo :]
            if way == 0:
                half = half + got[0, lo:mid].astype(F32)
            else:
                rest_of = rest_of + got[0, mid:hi].astype(F32)
            out[3, lo:mid] = half.astype(BF16)
            out[3, mid:hi] = rest_of.astype(BF16)
            launch(reduce_copy(chunk, 3, way))

    def reduce_end(chunk):
        lo, mid, hi = reduce_rows(chunk)
        total = pair_sum(chunk, 0)
        for slot in (2, 3):
            for way in (0, 1):
                reduce_copy(chunk, slot, way).wait_recv()
                total = total + (got_up, got_dn)[way][slot, lo:hi].astype(F32)
        final_ref[lo:hi] = total
        finished = jnp.concatenate(
            [final_ref[lo : lo + SPAN, j * LANE : (j + 1) * LANE].astype(BF16) for j in range(TILES)], axis=0
        )
        q = 0 if chunk else HALF
        send2[q : q + HALF] = mul(spill_ref[...], finished).astype(BF16).reshape(HALF, 16, LANE)
        if not chunk:
            recv2[OWN] = send2[OWN]
        exchange(send2, recv2, s2_s, s2_r, q, q + HALF, back=True)

    for load in loads[3:]:
        load.wait()
    near = run_expert(0)
    pair_begin(0)
    send_side(3)
    gather_end(1)
    reduce_begin(0)
    far = run_expert(1)
    pair_begin(1)
    reduce_middle(0)
    reduce_begin(1)

    stores = []

    def weight_gradient(n, ref, hbm, at, base):
        for f in range(4):
            ref[:, features(f)] = (
                mul_tn(near[at], unit_rows(base + f, 0)) + mul_tn(far[at], unit_rows(base + f, 1))
            ).astype(BF16)
        stores.append(pltpu.make_async_copy(ref, hbm.at[0], store_sem.at[n]))
        stores[-1].start()

    weight_gradient(0, gg_ref, gg_hbm, 1, 0)
    reduce_middle(1)
    reduce_end(0)
    weight_gradient(1, ug_ref, ug_hbm, 2, 0)
    weight_gradient(2, dg_ref, dg_hbm, 0, 4)
    reduce_end(1)

    arrived(side_recv, side_s, side_r, 0, PEERS)
    side_copy = remote(side_recv.at[:, :, LANE:], side_sib, pair_s.at[0], pair_r.at[0], at_expert(sibling))
    launch(side_copy)
    every = side_recv[...].reshape(PEERS * TOK, 2 * LANE)
    from_own = mul_tn(every[:, LANE:], every)
    side_copy.wait_recv()
    from_sib = mul_tn(side_sib[...].reshape(PEERS * TOK, LANE), every)
    for ref, mine_core, at in ((shared_gate_ref, 0, 0), (shared_up_ref, 0, UNITS), (shared_down_ref, 1, 2 * UNITS)):
        both = jnp.where(core == mine_core, from_own, from_sib)
        ref[...] = both[UNITS : UNITS + COLS, at : at + UNITS].astype(BF16)

    for copy in waits:
        copy.wait_send()
    waits.clear()
    sent(send1, s1_s, s1_r.at[0])
    sent(side_send, side_s, side_r)
    arrived(recv2, s2_s, s2_r, 0, PEERS)
    returned = recv2[...].reshape(rows, LANE)
    tokens = mul(back_hi_ref[...], returned) + mul(back_lo_ref[...], returned)
    shared_rows = jnp.concatenate(
        [final_ref[HALF_ROWS:, j * LANE : (j + 1) * LANE] for j in range(TILES)], axis=0
    )
    tok_ref[...] = tokens[: TILES * TOK] + shared_rows
    tok_copy = remote(tok_ref, tok_sib, pair_s.at[1], pair_r.at[1], at_expert(sibling))
    launch(tok_copy)
    tok_copy.wait_recv()
    summed = tok_ref[...] + tok_sib[...]
    full_ref[y] = summed.astype(BF16)
    for k in range(1, RING):
        other = ((y + k) % RING) * 2 + core
        launch(remote(full_ref.at[y], full_ref.at[y], e_s.at[k], e_r.at[k], at_expert(other)))

    terms = []
    for j in range(TILES):
        at = pl.ds(pl.multiple_of(quarter * QUARTER + j * LANE, LANE), LANE)
        terms.append(jnp.sum(summed[j * TOK : (j + 1) * TOK] * normalized_ref[:, at], axis=0, keepdims=True))
    line = jnp.concatenate(terms + [jnp.zeros((1, LANE), F32)], axis=1)
    for m in range(16):
        gain_send[m] = line[:, m * COLS : m * COLS + LANE]
    owner = (4 + x) * 2 + z // 8

    def gain_message(i):
        m = core * 8 + i
        peer = quarter * 16 + m
        return peer, remote(gain_send.at[m], gain_recv.at[(me + 2 * PEERS - 1 - peer) % PEERS], g_s.at[i], g_r, at_replica(peer))

    @pl.when(y >= 4)
    def send_gain():
        for i in range(8):
            peer, copy = gain_message(i)

            @pl.when(peer != me)
            def start():
                copy.start()

    @pl.when(expert == owner)
    def sum_gain():
        gain_recv[PEERS - 1] = gain_send[z]
        ref = gain_recv.at[: PEERS - 1]
        remote(ref, ref, g_s.at[0], g_r, at_replica((me + 1) % PEERS)).wait_recv()
        gain_all[...] = jnp.sum(gain_recv[...], axis=0)

        def tell(k, carry):
            other = (expert + k) % PARTS
            remote(gain_all, gain_all, gb_s.at[k], gb_r, at_expert(other)).start()
            return carry

        lax.fori_loop(1, PARTS, tell, 0)

    for k in range(1, RING):
        chip = (y + RING - k) % RING
        ref = full_ref.at[chip]
        remote(ref, ref, e_s.at[k], e_r.at[k], at_expert(chip * 2 + core)).wait_recv()

    def grad_tile(f, j):
        return full_ref[4 + f, j * TOK : (j + 1) * TOK, :].astype(F32)

    inner = jnp.zeros((TOK, LANE), F32)
    for f in range(4):
        for j in range(TILES):
            n = f * TILES + j
            inner = inner + grad_tile(f, j) * normalized_ref[:, feature_tile(f, j)] * gain_ref[n : n + 1, :]
    inner = jnp.sum(inner, axis=1, keepdims=True) * (1.0 / WIDTH)
    for f in range(4):
        for j in range(TILES):
            at, n = feature_tile(f, j), f * TILES + j
            moe_ref[:, at] = full_ref[f, j * TOK : (j + 1) * TOK, :]
            scaled = grad_tile(f, j) * gain_ref[n : n + 1, :]
            hidden_grad_ref[:, at] = (inv_rms * (scaled - normalized_ref[:, at] * inner)).astype(BF16)

    @pl.when(expert != owner)
    def take_gain():
        remote(gain_all, gain_all, gb_s.at[0], gb_r, at_expert(owner)).wait_recv()

    gain_grad_ref[...] = gain_all[...]

    for copy in waits:
        copy.wait_send()
    sent(send2, s2_s, s2_r)

    @pl.when(y >= 4)
    def gain_sent():
        for i in range(8):
            peer, copy = gain_message(i)

            @pl.when(peer != me)
            def wait():
                copy.wait_send()

    @pl.when(expert == owner)
    def told():
        def wait(k, carry):
            remote(gain_all, gain_all, gb_s.at[k], gb_r, at_expert((expert + k) % PARTS)).wait_send()
            return carry

        lax.fori_loop(1, PARTS, wait, 0)

    for store in stores:
        store.wait()


def hand_out(*refs):
    ins, outs, sems = refs[:9], refs[9:18], refs[18]
    copies = [pltpu.make_async_copy(src, dst, sems.at[n]) for n, (src, dst) in enumerate(zip(ins[:8], outs[:8]))]
    for copy in copies:
        copy.start()
    outs[8][...] = ins[8][0, :COLS]
    for copy in copies:
        copy.wait()


def per_device(
    hidden_in, norm_gain, expert_ids, gate_scores, w_gate, w_up, w_down, shared_gate, shared_up, shared_down, out_grad
):
    vmem, hbm = pl.BlockSpec(memory_space=pltpu.VMEM), pl.BlockSpec(memory_space=pl.ANY)
    dma = pltpu.SemaphoreType.DMA
    matrix = (UNITS, WIDTH)
    message = (PEERS, 16, LANE)
    tokens = jax.ShapeDtypeStruct((TOK, WIDTH), BF16)
    shared = jax.ShapeDtypeStruct((COLS, UNITS), BF16)
    weight = jax.ShapeDtypeStruct((1, UNITS, WIDTH), BF16)
    moe_out, hidden_grad, gain_grad, *grads = pl.pallas_call(
        layer_kernel,
        out_shape=(tokens, tokens, jax.ShapeDtypeStruct((1, LANE), F32), shared, shared, shared, weight, weight, weight),
        in_specs=[vmem] * 5 + [hbm] * 6,
        out_specs=[vmem] * 6 + [hbm] * 3,
        scratch_shapes=[pltpu.VMEM(matrix, BF16)] * 6
        + [
            dma((6,)),
            pltpu.VMEM((TOK, WIDTH), BF16),
            pltpu.VMEM((TOK, WIDTH), F32),
            pltpu.VMEM((LANE, PEERS * 16), BF16),
            pltpu.VMEM((LANE, PEERS * 16), BF16),
            pltpu.VMEM((TILES * SPAN, HALF * 16), BF16),
            pltpu.VMEM((HALF * 16, TILES * SPAN), BF16),
            pltpu.VMEM(message, BF16),
            pltpu.VMEM(message, BF16),
            pltpu.VMEM((RING, 2, HALF_ROWS, QUARTER), BF16),
            pltpu.VMEM((RING, 2, UNIT_ROWS, QUARTER), BF16),
            pltpu.VMEM((RING, UNIT_ROWS, QUARTER), BF16),
        ]
        + [pltpu.VMEM((4, UNIT_ROWS, QUARTER), BF16)] * 4
        + [
            pltpu.VMEM((UNIT_ROWS, QUARTER), F32),
            pltpu.VMEM((PEERS, TOK, 2 * LANE), BF16),
            pltpu.VMEM((PEERS, TOK, 2 * LANE), BF16),
            pltpu.VMEM((PEERS, TOK, LANE), BF16),
            pltpu.VMEM(message, BF16),
            pltpu.VMEM(message, BF16),
            pltpu.VMEM((TILES * TOK, LANE), F32),
            pltpu.VMEM((TILES * TOK, LANE), F32),
            pltpu.VMEM((RING, TILES * TOK, LANE), BF16),
            pltpu.VMEM((16, 1, LANE), F32),
            pltpu.VMEM((PEERS, 1, LANE), F32),
            pltpu.VMEM((1, LANE), F32),
        ]
        + [pltpu.VMEM(matrix, BF16)] * 3
        + [dma((3,))]
        + [dma, dma((2,)), dma, dma, dma, dma, dma((8,)), dma]
        + [dma((8,))] * 8
        + [dma((18,))] * 2
        + [dma((16,))] * 2
        + [dma((RING,))] * 2
        + [dma((PARTS,)), dma]
        + [dma((2,))] * 2,
        compiler_params=pltpu.CompilerParams(
            collective_id=0, has_side_effects=True, vmem_limit_bytes=56 * 1024 * 1024
        ),
    )(
        expert_ids.T,
        gate_scores.T,
        hidden_in,
        norm_gain.reshape(4 * TILES, LANE),
        out_grad,
        w_gate,
        w_up,
        w_down,
        shared_gate,
        shared_up,
        shared_down,
    )
    *copied, gain_grad = pl.pallas_call(
        hand_out,
        out_shape=(tokens, tokens, shared, shared, shared, weight, weight, weight, jax.ShapeDtypeStruct((COLS,), F32)),
        in_specs=[vmem] * 9,
        out_specs=[hbm] * 8 + [vmem],
        scratch_shapes=[dma((8,))],
    )(moe_out, hidden_grad, *grads, gain_grad)
    moe_out, hidden_grad, shared_gate_grad, shared_up_grad, shared_down_grad, *routed = copied
    return (
        moe_out, hidden_grad, gain_grad, *routed, shared_gate_grad.T, shared_up_grad.T, shared_down_grad.T
    )


def solution(mesh):
    rows, weights, shared = P("replica", None), P("replica", "expert", None), P("expert", None)
    return jax.shard_map(
        per_device,
        mesh=mesh,
        in_specs=(rows, P(), rows, rows, weights, weights, weights, shared, shared, shared, rows),
        out_specs=(rows, rows, P("replica"), weights, weights, weights) + (P("expert", "replica"),) * 3,
        check_vma=False,
    )
```

time: 152 us -> 123 us (0.81)
  Pallas kernels: 137 us -> 122 us
  local copies, waits for them, and re-layouts: 12.3 us -> 0 us
    pallas_call x1 -> x2, Pallas kernels: 137 us -> 122 us  [the longest x1 119 us: per_device(): pl.pallas_call(layer_kernel, out_shape=(tokens, tokens, jax.ShapeDtypeStr...]
    unnamed x16 -> x0, local copies, waits for them, and re-layouts: 8.99 us -> none
where the time goes in v2:
time: 123 us
  Pallas kernels  122 us (99%)
    pallas_call x1, Pallas kernels, per_device(): pl.pallas_call(layer_kernel, out_shape=(tokens, tokens, jax.ShapeDtypeStr...  119 us
    pallas_call x1, Pallas kernels, per_device(): pl.pallas_call(hand_out, out_shape=(tokens, tokens, shared, shared, share...  3.19 us

profile of v2, /device:TPU:1, one launch (start us, length us, event | category | flops | bytes accessed | tf_op | source)
XLA Modules:
  0.0 122.9 jit_solution(7785023696547183646)
XLA Ops:
  0.6 119.1 %shard_map.178 = (bf16[16,3584]{1,0:T(8,128)(2,1)}, bf16[16,3584]{1,0:T(8,128)(2,1)}, f32[1,128]{1,0:T(1,128)}, bf16[56,64]{1,0:T(8,128)(2,1)}, bf16[56,64]{1,0:...) custom-call(s32[8,16]{1,0:T(8,128)} %bitcast.7, ...), custom_call_target="tpu_custom_call" | custom-call | tf_op jit(solution)/shard_map/pallas_call | solution.py:628
  119.7 3.2 %shard_map.179 = (bf16[16,3584]{1,0:T(8,128)(2,1)}, bf16[16,3584]{1,0:T(8,128)(2,1)}, bf16[56,64]{1,0:T(8,128)(2,1)}, bf16[56,64]{1,0:T(8,128)(2,1)}, bf16[56,64...) custom-call(bf16[16,3584]{1,0:T(8,128)(2,1)} %get-tuple-element.27.r, ...), custom_call_target="tpu_custom_call" | custom-call | tf_op jit(solution)/shard_map/pallas_call | solution.py:688
